TPU v7x, 256 devices: a whole 4x4x8 slice. The times are simulated.
256 devices in a mesh: row: 32 (over z_hi, y, x), col: 8 (over z_lo, core).
Axes of the slice: x: 4, y: 4, z: 8 (z_hi: 2, z_lo: 4; z = z_hi * 4 + z_lo), core: 2. Of those that a mesh axis runs over, the one named last changes fastest.
Arguments:
- tokens: bfloat16 [5120, 3072], P('row', 'col'), may hold values from -6 to 6
- up_weight: bfloat16 [3072, 12288], P('row', 'col'), may hold values from -0.109375 to 0.109375
- down_weight: bfloat16 [12288, 3072], P('col', 'row'), may hold values from -0.0546875 to 0.0546875
Outputs:
- projected: bfloat16 [5120, 3072], P('row', 'col')
All inputs are finite; a program needn't handle non-finite values.
Results may differ from a plain program's by a relative error of at most 0.0049.
Values may be sent and summed in bfloat16 or wider, within the bound.
A program may use at most 128 MiB of HBM per device.

v0:
```python
import jax
import jax.numpy as jnp
from jax import lax
from jax.sharding import PartitionSpec as P


def add_panel(left, piece):
    return jnp.dot(left, piece, preferred_element_type=jnp.float32)


def local(tokens, up_weight, down_weight):
    token_rows = lax.all_gather(tokens, "col", axis=1, tiled=True)
    pre = add_panel(token_rows, lax.all_gather(up_weight, "row", axis=0, tiled=True))
    hidden = jax.nn.gelu(pre, approximate=False).astype(jnp.bfloat16)
    hidden_rows = lax.all_gather(hidden, "col", axis=1, tiled=True)
    full_rows = lax.all_gather(down_weight, "row", axis=1, tiled=True)
    down_cols = lax.all_to_all(full_rows, "col", split_axis=1, concat_axis=0, tiled=True)
    result = jnp.dot(hidden_rows, down_cols, preferred_element_type=jnp.float32)
    return result.astype(jnp.bfloat16)


def solution(mesh):
    return jax.shard_map(
        local,
        mesh=mesh,
        in_specs=(P("row", "col"), P("row", "col"), P("col", "row")),
        out_specs=P("row", "col"),
        check_vma=False,
    )
```

profile of v0, /device:TPU:1, one launch (start us, length us, event | category | flops | bytes accessed | tf_op | source)
XLA Modules:
  0.0 560.9 jit_solution(12348005389065564325)
XLA Ops:
  6.5 0.0 all-gather.8.cloned.1.call-start
  6.5 0.7 all-gather.8.cloned.1.call-update
  7.3 0.0 all-gather.4.cloned.1.call-start
  7.3 0.7 all-gather.4.cloned.1.call-update
  8.0 171.8 %all-gather.8.cloned.1.call-done = bf16[1536,3072]{0,1:T(8,128)(2,1)} async-done(((bf16[1536,96]{0,1:T(8,128)(2,1)}), bf16[1536,3072]{0,1:T(8,128)(2,1)}) %all-gather.8.cloned.1.call-update) | async-done | bytes 9437200 | tf_op jit(solution)/shard_map/all_gather | solution.py:16
  179.8 0.0 copy-start
  179.8 6.1 %all-to-all-start = ((bf16[1536,8,384]{0,2,1:T(8,128)(2,1)}), bf16[1536,8,384]{0,2,1:T(8,128)(2,1)}, u32[]{:S(2)}, u32[]{:S(2)}) async-start(bf16[1536,8,384]{0,2,1:T(8,128)(2,1)} %bitcast.8), calls=%async_computation | async-start | bytes 18874368 | tf_op jit(solution)/shard_map/all_to_all | solution.py:17
  185.9 0.0 all-gather.6.cloned.1.call-start
  185.9 0.0 copy-done
  185.9 304.7 %all_gather.12 = bf16[160,3072]{1,0:T(8,128)(2,1)S(1)} all-gather(bf16[160,384]{1,0:T(8,128)(2,1)S(1)} %copy-done), channel_id=1, replica_groups=mesh['row'=32,'col'=8] {'col'}, dimensions={1}, use_global_device_ids=true | all-gather | bytes 1105920 | tf_op jit(solution)/shard_map/all_gather | solution.py:12
  490.6 0.0 all-gather.4.cloned.1.call-done
  490.6 8.2 %fusion.2 = bf16[160,1536]{1,0:T(8,128)(2,1)} fusion(bf16[160,3072]{1,0:T(8,128)(2,1)S(1)} %all_gather.12, bf16[3072,1536]{1,0:T(8,128)(2,1)} %all-gather.4.cloned.1.call-done), kind=kOutput, calls=%fused_computation.4 | convolution fusion | flops 1525923840 | bytes 10911744 | tf_op jit(solution)/shard_map/dot_general | solution.py:8
  498.8 0.0 all-gather.6.cloned.1.call-update
  498.8 0.0 all-to-all-done
  498.8 12.6 %copy.4 = bf16[8,1536,384]{2,1,0:T(8,128)(2,1)} copy(bf16[8,1536,384]{1,2,0:T(8,128)(2,1)} %bitcast.1) | data formatting | bytes 18874368 | tf_op jit(solution)/shard_map/all_to_all | solution.py:17
  511.4 35.2 %all-gather.6.cloned.1.call-done = bf16[160,12288]{1,0:T(8,128)(2,1)} async-done(((bf16[160,1536]{1,0:T(8,128)(2,1)}), bf16[160,12288]{1,0:T(8,128)(2,1)}) %all-gather.6.cloned.1.call-update) | async-done | bytes 3932176 | tf_op jit(solution)/shard_map/all_gather | solution.py:15
  546.6 7.7 %convolution_convert_fusion = bf16[160,384]{1,0:T(8,128)(2,1)} fusion(bf16[160,12288]{1,0:T(8,128)(2,1)} %all-gather.6.cloned.1.call-done, bf16[12288,384]{1,0:T(8,128)(2,1)} %bitcast.7), kind=kOutput, calls=%fused_computation.1 | convolution fusion | flops 1510010880 | bytes 13492224 | tf_op jit(solution)/shard_map/dot_general | solution.py:18
Async XLA Ops:
  6.5 173.2 %all-gather.8.cloned.1.call-start = ((), (), s32[]{:S(2)}) async-start(), calls=%async_computation.3 | async-start | bytes 9732096 | tf_op jit(solution)/shard_map/all_gather | solution.py:16
  7.3 483.4 %all-gather.4.cloned.1.call-start = ((), (), s32[]{:S(2)}) async-start(), calls=%async_computation.1 | async-start | bytes 9732096 | tf_op jit(solution)/shard_map/all_gather | solution.py:13
  179.8 6.2 %copy-start = (bf16[160,384]{1,0:T(8,128)(2,1)S(1)}, bf16[160,384]{1,0:T(8,128)(2,1)}, u32[]{:S(2)}) copy-start(bf16[160,384]{1,0:T(8,128)(2,1)} %param.3) | copy-start | bytes 368644
  179.8 319.0 %all-to-all-start = ((bf16[1536,8,384]{0,2,1:T(8,128)(2,1)}), bf16[1536,8,384]{0,2,1:T(8,128)(2,1)}, u32[]{:S(2)}, u32[]{:S(2)}) async-start(bf16[1536,8,384]{0,2,1:T(8,128)(2,1)} %bitcast.8), calls=%async_computation | async-start | bytes 18874368 | tf_op jit(solution)/shard_map/all_to_all | solution.py:17
  185.9 360.7 %all-gather.6.cloned.1.call-start = ((), (), s32[]{:S(2)}) async-start(), calls=%async_computation.2 | async-start | bytes 4423680 | tf_op jit(solution)/shard_map/all_gather | solution.py:15
Sparse Core Ops, SparseCore 0:
  10.7 168.9 all-gather.7
  183.2 232.6 all-gather.3
  498.9 47.6 all-gather.5
where the time goes:
time: 563 us; the launch traced here: 561 us
  blocking collectives  305 us (54%)
  waiting for transfers between devices  208 us (37%)
  matrix products  15.9 us (3%)
  between operations  13.1 us (2%)
  local copies, waits for them, and re-layouts  12.6 us (2%)
  starting transfers between devices  6.19 us (1%)
    all_gather x1, blocking collectives, local(): token_rows = lax.all_gather(tokens, 'col', axis=1, tiled=True)  305 us
    all_gather x1, waiting for transfers between devices, local(): full_rows = lax.all_gather(down_weight, 'row', axis=1, tiled=True)  172 us
    all_gather x1, waiting for transfers between devices, local(): hidden_rows = lax.all_gather(hidden, 'col', axis=1, tiled=True)  35.2 us
    all_to_all x1, local copies, waits for them, and re-layouts, local(): lax.all_to_all(full_rows, 'col', split_axis=1, concat_axis=0, tiled=True)  12.6 us
  transfers between devices with their start and end apart: 4, of which 2 were waited for; matrix products, arithmetic and copies ran while one was open for 4% of the time, Pallas kernels for 0%

commit v1 on v0

v1 whole, which is shorter than its diff:
```python
import jax
import jax.numpy as jnp
from jax import lax
from jax.experimental import pallas as pl
from jax.experimental.pallas import tpu as pltpu
from jax.sharding import PartitionSpec as P

MESH = pl.DeviceIdType.MESH
BF = jnp.bfloat16
F32 = jnp.float32
R0, R1 = 32, 48
SEMS = 200


def dev(x, y, z, k):
    return ((z // 4) * 16 + y * 4 + x, (z % 4) * 2 + k)


def body(tok, up, dn, out, T, U, D, dnT, acc, H, O, Ls, Lr, S0, Q0, S1, Q1, V0, f0s, f0r, fin, finr, ss, rs):
    row = lax.axis_index("row")
    col = lax.axis_index("col")
    x, y, zh = row % 4, (row // 4) % 4, row // 16
    zl, k = col // 2, col % 2
    z = 4 * zh + zl
    hi, lo = x // 2, x % 2
    yh, yl = y // 2, y % 2
    turn = ((x + 1) // 2) % 2
    here = (x, y, z, k)
    at_core = dev(x, y, z, 1 - k)
    at_lo = dev(2 * hi + 1 - lo, y, z, k)
    at_x = dev(3 - x, y, z, k)
    at_a = dev(x, 2 * yh + 1 - yl, z, k)
    at_b = dev(x, 3 - y, z, k)
    at_z = (dev(x, y, (z + 1) % 8, k), dev(x, y, (z + 7) % 8, k))

    barrier = pltpu.get_barrier_semaphore()
    friends = [at_x, at_a, at_b, at_z[0], at_z[1]]
    for fx in (0, 1):
        for fz in (0, 1):
            for fk in (0, 1):
                if fx or fz or fk:
                    friends.append(dev(2 * hi + (1 - lo if fx else lo), y, (z + 4 * fz) % 8, 1 - k if fk else k))
    for f in friends:
        pl.semaphore_signal(barrier, inc=1, device_id=f, device_id_type=MESH)
    pl.semaphore_wait(barrier, len(friends))

    count = [0]
    pending = []

    def slots(n):
        first = count[0]
        count[0] += n
        assert count[0] <= SEMS
        return first

    def copy(src, dst, to, i, j=None):
        return pltpu.make_async_remote_copy(
            src_ref=src, dst_ref=dst, send_sem=ss.at[i], recv_sem=rs.at[i if j is None else j],
            device_id=to, device_id_type=MESH)

    def send(src, dst, to, i):
        c = copy(src, dst, to, i)
        c.start()
        pending.append(c.wait_send)
        return c

    def landed(ref, i):
        pltpu.make_async_copy(ref, ref, rs.at[i]).wait()

    lane = pl.ds(pl.multiple_of(k * 384, 128), 384)

    def spread(S, B):
        base = slots(4)
        far = zh + k - 2 * zh * k
        for g in (0, 1):
            for h in (0, 1):
                src = S.at[:, pl.ds((2 * g + h) * 384, 384)]
                dst = B.at[zh, y, x, :, pl.ds(h * 384, 384)]
                to = dev(2 * hi + (1 - hi if g else hi), y, 4 * k + zl, h)
                own = (far == 0) & (turn == g) & (k == h)

                def c(src=src, dst=dst, to=to, i=base + 2 * g + h):
                    return copy(src, dst, to, i, base + 2 * far + lo)

                @pl.when(own)
                def _():
                    pltpu.make_async_copy(src, dst, rs.at[base + 2 * far + lo]).start()

                @pl.when(jnp.logical_not(own))
                def _():
                    c().start()

                def done(own=own, c=c):
                    @pl.when(jnp.logical_not(own))
                    def _():
                        c().wait_send()
                pending.append(done)

        def arrived(zs):
            off = zs + zh - 2 * zs * zh
            for l in (0, 1):
                landed(B.at[zs, y, 2 * hi + l, :, lane], base + 2 * off + l)
        return arrived

    def gather(B, zs):
        pair, ypair = pl.ds(2 * hi, 2), pl.ds(2 * yh, 2)
        every = pl.ds(0, 4)

        def sl(ys, xs, p):
            return B.at[zs, ys, xs, pl.ds(32 * p, 32), lane]

        plan = (
            ((at_x, 0, ((y, pair),)), (at_a, 1, ((y, pair),)), (at_b, 2, ((y, pair),))),
            ((at_a, 0, ((y, every),)), (at_b, 1, ((ypair, pair),)), (at_x, 2, ((y, pair), (3 - y, pair)))),
            ((at_b, 0, ((ypair, every),)), (at_x, 1, ((every, pair),)), (at_a, 2, ((y, every), (3 - y, every)))),
        )
        live = {}

        def go(step):
            cs = []
            for to, p, sets in plan[step]:
                for ys, xs in sets:
                    r = sl(ys, xs, p)
                    cs.append(send(r, r, to, slots(1)))
            live[step] = cs

        def wait(step):
            for c in live[step]:
                c.wait_recv()

        def forward():
            r = B.at[zs, :, :, :, lane]
            live["f"] = [send(r, r, at_core, slots(1))]
        return go, wait, forward

    def t_most(st, dr):
        return 4 if st == dr else 3

    def t_slice(zo, st):
        if st == 0:
            return T.at[zo % 4, pl.ds(2 * (zo // 4), 2), pl.ds(0, R0)]
        return T.at[zo % 4, 2 * (zo // 4) + lo, pl.ds(R0, R1)]

    t_live, lo_live = {}, []

    def t_origin(dr, d):
        return (z + 8 - d) % 8 if dr == 0 else (z + d) % 8

    def t_send(st, d):
        for dr in (0, 1):
            if d <= t_most(st, dr):
                r = t_slice(t_origin(dr, d - 1), st)
                t_live[st, dr, d] = send(r, r, at_z[dr], slots(1))

    def t_wait(st, d):
        for dr in (0, 1):
            if d <= t_most(st, dr):
                t_live[st, dr, d].wait_recv()
                if st == 1:
                    t_to_lo(t_origin(dr, d))

    def t_to_lo(zo):
        r = t_slice(zo, 1)
        lo_live.append(send(r, r, at_lo, slots(1)))

    up_arrived = spread(up, U)
    q_own = 2 * zh + lo
    rows_of = lambda c: pl.ds(pl.multiple_of(c * 80, 16), 80)
    tx = slots(1)
    t_dst = T.at[zl, q_own, :, lane]
    tc = copy(tok.at[rows_of(1 - k)], t_dst, at_core, tx)
    tc.start()
    pending.append(tc.wait_send)
    i = slots(1)
    own_copy = pltpu.make_async_copy(tok.at[rows_of(k)], t_dst, rs.at[i])
    own_copy.start()

    eye = (lax.broadcasted_iota(jnp.int32, (96, 96), 0) == lax.broadcasted_iota(jnp.int32, (96, 96), 1)).astype(BF)
    dnT[...] = lax.dot_general(eye, dn[...], (((1,), (1,)), ((), ())), preferred_element_type=F32).astype(BF)

    own_copy.wait()
    tc.wait_recv()
    i = slots(1)
    r = T.at[zl, q_own, pl.ds(0, R0)]
    lo0 = send(r, r, at_lo, i)
    t_send(1, 1)
    t_to_lo(z)
    dn_arrived = spread(dnT, D)

    un, uf = gather(U, zh), gather(U, 1 - zh)
    d0, d1 = gather(D, 0), gather(D, 1)
    GO, WAIT, FWD = 0, 1, 2

    up_arrived(zh)
    un[GO](0)
    lo0.wait_recv()
    t_send(0, 1)
    un[WAIT](0)
    un[GO](1)
    t_wait(1, 1)
    t_send(1, 2)
    t_wait(0, 1)
    t_send(0, 2)
    un[WAIT](1)
    un[GO](2)
    up_arrived(1 - zh)
    uf[GO](0)
    t_wait(1, 2)
    t_send(1, 3)
    t_wait(0, 2)
    t_send(0, 3)
    uf[WAIT](0)
    uf[GO](1)
    dn_arrived(0)
    d0[GO](0)
    un[WAIT](2)
    un[FWD]()
    t_wait(1, 3)
    t_send(1, 4)
    t_wait(0, 3)
    t_send(0, 4)
    uf[WAIT](1)
    uf[GO](2)
    d0[WAIT](0)
    d0[GO](1)
    dn_arrived(1)
    d1[GO](0)
    t_wait(1, 4)
    t_wait(0, 4)
    d0[WAIT](1)
    d0[GO](2)
    d1[WAIT](0)
    uf[WAIT](2)
    uf[FWD]()
    d1[GO](1)
    for c in lo_live:
        c.wait_recv()
    un[WAIT]("f")
    uf[WAIT]("f")

    acc[...] = jnp.zeros_like(acc)

    def up_step(j, carry):
        acc[...] += jnp.dot(
            T[j].reshape(320, 768), U[j // 2, pl.ds(2 * (j % 2), 2)].reshape(768, 768), preferred_element_type=F32)
        return carry
    lax.fori_loop(0, 4, up_step, 0)

    def act(j, carry):
        r = pl.ds(pl.multiple_of(j * 32, 32), 32)
        v = acc[r, :]
        H[r, :] = (v * (1.0 + lax.erf(v * 0.7071067811865476)) * 0.5).astype(BF)
        return carry
    lax.fori_loop(0, 10, act, 0)

    def project(phi):
        for j in (0, 1):
            w = D[phi, 2 * j:2 * j + 2].reshape(768, 768)
            o = lax.dot_general(H[...], w, (((1,), (1,)), ((), ())), preferred_element_type=F32)
            O[2 * phi + j] = o.reshape(4, 80, 768)

    l_base = slots(8)
    r_base = {}
    for phi in (0, 1):
        for st in (0, 1):
            for dr in (0, 1):
                r_base[phi, st, dr] = slots(4)

    def l_copy(t):
        i = l_base + t
        return copy(Ls.at[t], Lr.at[t], at_lo, i)

    def l_send(phi):
        for off in (4, 3, 5, 2, 6, 1, 7, 0):
            t = (z + off) % 8

            @pl.when((t % 4) // 2 == phi)
            def _():
                Ls[t] = O[t % 4, 2 * (t // 4) + 1 - lo, R0:].astype(BF)
                l_copy(t).start()

            def done(t=t):
                @pl.when((t % 4) // 2 == phi)
                def _():
                    l_copy(t).wait_send()
            pending.append(done)

    def ring_copy(phi, st, dr, d):
        i = r_base[phi, st, dr] + d - 1
        S, Q = ((S0, Q0), (S1, Q1))[st]
        n = ((phi * 2 + dr) * 4) + d - 1
        return copy(S.at[n], Q.at[n], at_z[dr], i)

    def term(st, t):
        if st == 0:
            return O[t % 4, pl.ds(2 * (t // 4), 2), 0:R0]
        l_copy(t).wait_recv()
        return O[t % 4, 2 * (t // 4) + lo, R0:] + Lr[t].astype(F32)

    def ring(phi, st, d):
        for dr in (0, 1):
            if d > t_most(st, dr):
                continue
            t = (z + d) % 8 if dr == 0 else (z + 8 - d) % 8
            S, Q = ((S0, Q0), (S1, Q1))[st]

            @pl.when((t % 4) // 2 == phi)
            def _():
                v = term(st, t)
                if d < t_most(st, dr):
                    ring_copy(phi, st, dr, d + 1).wait_recv()
                    v = v + Q[(phi * 2 + dr) * 4 + d].astype(F32)
                S[(phi * 2 + dr) * 4 + d - 1] = v.astype(BF)
                ring_copy(phi, st, dr, d).start()

            def done(t=t, dr=dr):
                @pl.when((t % 4) // 2 == phi)
                def _():
                    ring_copy(phi, st, dr, d).wait_send()
            pending.append(done)

    f_i, c_i = slots(1), slots(1)

    def own_total(phi, st):
        v = term(st, z)
        Q = (Q0, Q1)[st]
        for dr in (0, 1):
            ring_copy(phi, st, dr, 1).wait_recv()
            v = v + Q[(phi * 2 + dr) * 4].astype(F32)
        return v

    f_copy = copy(f0s, f0r, at_lo, f_i)
    c_copy = copy(fin.at[1 - k], finr, at_core, c_i)

    def finish(phi):
        @pl.when((z % 4) // 2 == phi)
        def _():
            V0[...] = own_total(phi, 0)
            f0s[...] = V0[1 - lo].astype(BF)
            f_copy.start()
            w = own_total(phi, 1).astype(BF)
            fin[0, R0:] = w[:, :384]
            fin[1, R0:] = w[:, 384:]
            f_copy.wait_recv()
            w = (V0[lo] + f0r[...].astype(F32)).astype(BF)
            fin[0, 0:R0] = w[:, :384]
            fin[1, 0:R0] = w[:, 384:]
            c_copy.start()
            out[k] = fin[k]

    d0[WAIT](2)
    d0[FWD]()
    d1[WAIT](1)
    d1[GO](2)
    d0[WAIT]("f")
    project(0)
    l_send(0)
    ring(0, 0, 4)
    ring(0, 1, 4)
    ring(0, 0, 3)
    ring(0, 1, 3)
    d1[WAIT](2)
    d1[FWD]()
    ring(0, 0, 2)
    ring(0, 1, 2)
    d1[WAIT]("f")
    project(1)
    l_send(1)
    ring(1, 0, 4)
    ring(1, 1, 4)
    ring(0, 0, 1)
    ring(0, 1, 1)
    ring(1, 0, 3)
    ring(1, 1, 3)
    ring(1, 0, 2)
    ring(1, 1, 2)
    ring(1, 0, 1)
    ring(1, 1, 1)
    finish(0)
    finish(1)
    c_copy.wait_recv()
    out[1 - k] = finr[...]
    pending.append(f_copy.wait_send)
    pending.append(c_copy.wait_send)
    for w in pending:
        w()


def local(tokens, up_weight, down_weight):
    vmem = pl.BlockSpec(memory_space=pltpu.VMEM)
    out = pl.pallas_call(
        body,
        out_shape=jax.ShapeDtypeStruct((2, 80, 384), BF),
        in_specs=[vmem] * 3,
        out_specs=vmem,
        scratch_shapes=[
            pltpu.VMEM((4, 4, 80, 768), BF),
            pltpu.VMEM((2, 4, 4, 96, 768), BF),
            pltpu.VMEM((2, 4, 4, 96, 768), BF),
            pltpu.VMEM((96, 1536), BF),
            pltpu.VMEM((320, 768), F32),
            pltpu.VMEM((320, 768), BF),
            pltpu.VMEM((4, 4, 80, 768), F32),
            pltpu.VMEM((8, R1, 768), BF),
            pltpu.VMEM((8, R1, 768), BF),
            pltpu.VMEM((16, 2, R0, 768), BF),
            pltpu.VMEM((16, 2, R0, 768), BF),
            pltpu.VMEM((16, R1, 768), BF),
            pltpu.VMEM((16, R1, 768), BF),
            pltpu.VMEM((2, R0, 768), F32),
            pltpu.VMEM((R0, 768), BF),
            pltpu.VMEM((R0, 768), BF),
            pltpu.VMEM((2, 80, 384), BF),
            pltpu.VMEM((80, 384), BF),
            pltpu.SemaphoreType.DMA((SEMS,)),
            pltpu.SemaphoreType.DMA((SEMS,)),
        ],
        compiler_params=pltpu.CompilerParams(
            collective_id=0, has_side_effects=True, vmem_limit_bytes=48 << 20),
        name="ffn",
    )(tokens, up_weight, down_weight)
    return out.reshape(160, 384)


def solution(mesh):
    return jax.shard_map(
        local,
        mesh=mesh,
        in_specs=(P("row", "col"), P("row", "col"), P("col", "row")),
        out_specs=P("row", "col"),
        check_vma=False,
    )
```

time: 563 us -> 101 us (0.18)
  blocking collectives: 305 us -> 0 us
  waiting for transfers between devices: 208 us -> 0 us
  Pallas kernels: 0 us -> 98 us
  matrix products: 15.9 us -> 0 us
  between operations: 13.1 us -> 0.03 us
  local copies, waits for them, and re-layouts: 12.6 us -> 1.89 us
  starting transfers between devices: 6.19 us -> 0 us
    all_gather x1 -> x0, blocking collectives: 305 us -> none  [local(): token_rows = lax.all_gather(tokens, 'col', axis=1, tiled=True)]
    all_gather x3 -> x0, waiting for transfers between devices: 207 us -> none  [the longest x1 172 us: local(): full_rows = lax.all_gather(down_weight, 'row', axis=1, tiled=True)]
    pallas_call x0 -> x1, Pallas kernels: none -> 98 us  [local(): pl.pallas_call(body, out_shape=jax.ShapeDtypeStruct((2, 80, 384), BF), in...]
    dot_general x2 -> x0, matrix products: 15.9 us -> none  [the longest x1 8.16 us: add_panel(): return jnp.dot(left, piece, preferred_element_type=jnp.float32)]
    all_to_all x1 -> x0, local copies, waits for them, and re-layouts: 12.6 us -> none  [local(): lax.all_to_all(full_rows, 'col', split_axis=1, concat_axis=0, tiled=True)]
    all_to_all x1 -> x0, starting transfers between devices: 6.15 us -> none  [local(): lax.all_to_all(full_rows, 'col', split_axis=1, concat_axis=0, tiled=True)]
  transfers between devices with their start and end apart: 4 -> 0, of which waited for: 2 -> 0; matrix products, arithmetic and copies ran while one was open for 4% -> 0% of each run, Pallas kernels for 0% -> 0%
where the time goes in v1:
time: 101 us; the launch traced here: 99.9 us
  Pallas kernels  98 us (97%)
  local copies, waits for them, and re-layouts  1.89 us (2%)
    pallas_call x1, Pallas kernels, local(): pl.pallas_call(body, out_shape=jax.ShapeDtypeStruct((2, 80, 384), BF), in...  98 us

profile of v1, /device:TPU:1, one launch (start us, length us, event | category | flops | bytes accessed | tf_op | source)
XLA Modules:
  0.0 99.9 jit_solution(12252086854411708573)
XLA Ops:
  0.0 0.0 copy-start
  0.0 0.0 copy-start.1
  0.0 1.2 %copy.4.dn = bf16[1536,96]{1,0:T(8,128)(2,1)S(1)} copy(bf16[1536,96]{0,1:T(8,128)(2,1)} %param.5) | data formatting | bytes 589824 | tf_op args[2]
  1.2 0.0 copy-done
  1.3 0.0 copy-done.1
  1.3 98.0 %ffn.1 = bf16[2,80,384]{2,1,0:T(8,128)(2,1)S(1)} custom-call(bf16[160,384]{1,0:T(8,128)(2,1)S(1)} %copy-done.1, bf16[96,1536]{1,0:T(8,128)(2,1)S(1)} %copy-done, bf16[1536,96]{1,0:T(8,128)(2,1)S(1)} %copy.4.dn), custom_call_target="tpu_custom_call" | custom-call | tf_op jit(solution)/shard_map/ffn/pallas_call | solution.py:391
  99.3 0.7 copy.6
Async XLA Ops:
  0.0 1.2 %copy-start = (bf16[96,1536]{1,0:T(8,128)(2,1)S(1)}, bf16[96,1536]{1,0:T(8,128)(2,1)}, u32[]{:S(2)}) copy-start(bf16[96,1536]{1,0:T(8,128)(2,1)} %up.1) | copy-start | bytes 884740
  0.0 1.3 %copy-start.1 = (bf16[160,384]{1,0:T(8,128)(2,1)S(1)}, bf16[160,384]{1,0:T(8,128)(2,1)}, u32[]{:S(2)}) copy-start(bf16[160,384]{1,0:T(8,128)(2,1)} %tok.1) | copy-start | bytes 368644

commit v2 on v0

v2 whole, which is shorter than its diff:
```python
import jax
import jax.numpy as jnp
from jax import lax
from jax.experimental import pallas as pl
from jax.experimental.pallas import tpu as pltpu
from jax.sharding import PartitionSpec as P

MESH = pl.DeviceIdType.MESH
BF = jnp.bfloat16
F32 = jnp.float32
TA, TB = 32, 48
SEMS = 280


def dev(x, y, z, k):
    return ((z // 4) * 16 + y * 4 + x, (z % 4) * 2 + k)


def body(tok, up, dn, out, T, U, D, acc, H, O, S, Q, F, SO, OA, V, E, ss, rs):
    row = lax.axis_index("row")
    col = lax.axis_index("col")
    x, y, zh = row % 4, (row // 4) % 4, row // 16
    zl, k = col // 2, col % 2
    z = 4 * zh + zl
    hi, lo = x // 2, x % 2
    yh, yl = y // 2, y % 2
    ya = 2 * yh + 1 - yl
    turn = ((x + 1) // 2) % 2
    x_lo = 2 * hi + 1 - lo

    def ring_z(n):
        return (z + 8 + n) % 8

    at_core = dev(x, y, z, 1 - k)
    at_lo = dev(x_lo, y, z, k)
    at_x = dev(3 - x, y, z, k)
    at_a = dev(x, ya, z, k)
    at_b = dev(x, 3 - y, z, k)
    at_z = (dev(x, y, ring_z(1), k), dev(x, y, ring_z(-1), k))

    barrier = pltpu.get_barrier_semaphore()
    friends = [at_x, at_a, at_b]
    for n in (0, 4, 1, -1):
        for px in (x, x_lo):
            for pk in (k, 1 - k):
                if n or px is not x or pk is not k:
                    friends.append(dev(px, y, ring_z(n), pk))
    for f in friends:
        pl.semaphore_signal(barrier, inc=1, device_id=f, device_id_type=MESH)
    pl.semaphore_wait(barrier, len(friends))

    count = [0]
    pending = []

    def slots(n):
        first = count[0]
        count[0] += n
        assert count[0] <= SEMS
        return first

    def copy(src, dst, to, i, j=None):
        return pltpu.make_async_remote_copy(
            src_ref=src, dst_ref=dst, send_sem=ss.at[i], recv_sem=rs.at[i if j is None else j],
            device_id=to, device_id_type=MESH)

    def send(src, dst, to, i=None, j=None):
        c = copy(src, dst, to, slots(1) if i is None else i, j)
        c.start()
        pending.append(c.wait_send)
        return c

    def landed(ref, i):
        pltpu.make_async_copy(ref, ref, rs.at[i]).wait()

    def spread(S, at):
        base = slots(4)
        far = zh + k - 2 * zh * k
        for g in (0, 1):
            for h in (0, 1):
                src = S.at[..., pl.ds((2 * g + h) * 384, 384)]
                dst = at(h, zh, x)
                to = dev(2 * hi + (1 - hi if g else hi), y, 4 * k + zl, h)
                own = (far == 0) & (turn == g) & (k == h)

                def c(src=src, dst=dst, to=to, i=base + 2 * g + h):
                    return copy(src, dst, to, i, base + 2 * far + lo)

                @pl.when(own)
                def _():
                    pltpu.make_async_copy(src, dst, rs.at[base + 2 * far + lo]).start()

                @pl.when(jnp.logical_not(own))
                def _():
                    c().start()

                def done(own=own, c=c):
                    @pl.when(jnp.logical_not(own))
                    def _():
                        c().wait_send()
                pending.append(done)

        def arrived(zs):
            off = zs + zh - 2 * zs * zh
            for l in (0, 1):
                landed(at(k, zs, 2 * hi + l), base + 2 * off + l)
        return arrived

    pair, other = pl.ds(2 * hi, 2), pl.ds(2 - 2 * hi, 2)
    ypair, yother = pl.ds(2 * yh, 2), pl.ds(2 - 2 * yh, 2)
    every = pl.ds(0, 4)
    plan = (
        ((at_x, 0, ((y, pair),)), (at_a, 1, ((y, pair),)), (at_b, 2, ((y, pair),))),
        ((at_a, 0, ((y, every),)), (at_b, 1, ((ypair, pair),)), (at_x, 2, ((y, pair), (3 - y, pair)))),
        ((at_b, 0, ((ypair, every),)), (at_x, 1, ((every, pair),)), (at_a, 2, ((y, every), (3 - y, every)))),
    )
    held = tuple((p, s) for _, p, s in plan[2])
    last = ((0, ((yother, every),)), (1, ((every, other),)), (2, ((ya, every), (3 - ya, every))))

    class Gather:
        def __init__(self, part):
            self.part, self.live = part, {}

        def go(self, step):
            rs_ = [(to, self.part(ys, xs, p)) for to, p, sets in plan[step] for ys, xs in sets]
            self.live[step] = [send(r, r, to) for to, r in rs_]

        def wait(self, step):
            for c in self.live[step]:
                c.wait_recv()

        def forward(self, what):
            rs_ = [self.part(ys, xs, p) for p, sets in what for ys, xs in sets]
            self.live["f"] = self.live.get("f", []) + [send(r, r, at_core) for r in rs_]

    def up_part(zs):
        return lambda ys, xs, p: U.at[k, zs, ys, xs, pl.ds(32 * p, 32)]

    def dn_part(zs):
        return lambda ys, xs, p: D.at[:, k, zs, ys, xs, :, pl.ds(128 * p, 128)]

    def dn_last(b):
        return lambda ys, xs, p: D.at[b, k, :, ys, xs, :, pl.ds(128 * p, 128)]

    def most(st, dr):
        return 4 if st == dr else 3

    def t_slice(zo, st):
        if st == 0:
            return T.at[zo % 4, pl.ds(2 * (zo // 4), 2), pl.ds(0, TA)]
        return T.at[zo % 4, 2 * (zo // 4) + lo, pl.ds(TA, TB)]

    t_live, lo_live = {}, []

    def t_origin(dr, d):
        return ring_z(-d if dr == 0 else d)

    def t_send(st, d):
        for dr in (0, 1):
            if d <= most(st, dr):
                r = t_slice(t_origin(dr, d - 1), st)
                t_live[st, dr, d] = send(r, r, at_z[dr])

    def t_wait(st, d):
        for dr in (0, 1):
            if d <= most(st, dr):
                t_live[st, dr, d].wait_recv()
                if st == 1:
                    t_to_lo(t_origin(dr, d))

    def t_to_lo(zo):
        r = t_slice(zo, 1)
        lo_live.append(send(r, r, at_lo))

    def project(b):
        w = jnp.concatenate([D[b, h].reshape(1024, 384) for h in (0, 1)], axis=1)
        o = lax.dot_general(H[...], w, (((1,), (1,)), ((), ())), preferred_element_type=F32)
        for j in range(8):
            O[b, j // 2, j % 2] = o[:, 128 * j:128 * j + 128].reshape(4, 80, 128)

    ring_base = slots(24)
    last_send, last_recv = slots(24), slots(24)
    own_send, own_recv = slots(9), slots(12)

    def far_dir(b, dr):
        return b % 2 == dr

    def ring_copies(b, dr, d):
        n = (b * 2 + dr) * 4
        src = S.at[n + d - 1]
        if d > 1:
            return [copy(src, Q.at[n + d - 1], at_z[dr], ring_base + n + d - 1)]
        zt = ring_z(1 if dr == 0 else -1)
        return [copy(src.at[c, l], F.at[b, dr, k, lo], dev(2 * hi + l, y, zt, c),
                     last_send + n + 2 * c + l, last_recv + n + 2 * k + lo)
                for c in (0, 1) for l in (0, 1)]

    def ring(b, step):
        for dr in (0, 1):
            first = 4 if far_dir(b, dr) else 3
            d = first - step
            if d == 0:
                continue
            t = ring_z(d if dr == 0 else -d)
            n = (b * 2 + dr) * 4
            v = O[b, t % 4, :, pl.ds(2 * (t // 4), 2)]
            if step:
                ring_copies(b, dr, d + 1)[0].wait_recv()
                v = v + Q[n + d].astype(F32)
            S[n + d - 1] = v.astype(BF)
            for c in ring_copies(b, dr, d):
                c.start()
                pending.append(c.wait_send)

    def own(b):
        SO[b] = O[b, zl, :, pl.ds(2 * zh, 2)].astype(BF)
        for i, (l, c) in enumerate(((lo, 1 - k), (1 - lo, k), (1 - lo, 1 - k))):
            send(SO.at[b, c, l], OA.at[b, k, lo], dev(2 * hi + l, y, z, c), own_send + 3 * b + i, own_recv + 4 * b + 2 * k + lo)

    def up32(r):
        return r.astype(F32)

    def finish(b):
        for l in (0, 1):
            landed(OA.at[b, 1 - k, l], own_recv + 4 * b + 2 * (1 - k) + l)
        landed(OA.at[b, k, 1 - lo], own_recv + 4 * b + 2 * k + 1 - lo)
        for kk in (1 - k, k):
            if kk is k:
                v = O[b, zl, k, 2 * zh + lo] + up32(OA[b, k, 1 - lo])
            else:
                v = up32(OA[b, kk, 0]) + up32(OA[b, kk, 1])
            for dr in (0, 1):
                for l in (0, 1):
                    landed(F.at[b, dr, kk, l], last_recv + (b * 2 + dr) * 4 + 2 * kk + l)
                    v = v + up32(F[b, dr, kk, l])
            V[kk, :, 128 * b:128 * b + 128] = v.astype(BF)

    def order():
        i = lax.broadcasted_iota(jnp.int32, (384, 384), 0)
        j = lax.broadcasted_iota(jnp.int32, (384, 384), 1)
        E[...] = (j == 96 * ((i % 128) // 32) + 32 * (i // 128) + i % 32).astype(F32).astype(BF)

    def pre():
        for h in (0, 1):
            v = None
            for j in range(4):
                o = jnp.dot(T[j].reshape(320, 768), U[h, j // 2, 2 * (j % 2):2 * (j % 2) + 2].reshape(768, 384),
                            preferred_element_type=F32)
                v = o if v is None else v + o
            acc[h] = v

    def act(j, carry):
        r = pl.ds(pl.multiple_of(j * 80, 16), 80)
        for h in (0, 1):
            v = acc[h, r, :]
            H[r, h * 384:(h + 1) * 384] = (v * (1.0 + lax.erf(v * 0.7071067811865476)) * 0.5).astype(BF)
        return carry

    up_arrived = spread(up, lambda h, zs, xs: U.at[h, zs, y, xs])

    def rows_of(c):
        return pl.ds(pl.multiple_of(c * 80, 16), 80)

    lane = pl.ds(pl.multiple_of(k * 384, 128), 384)
    q_own = 2 * zh + lo
    t_dst = T.at[zl, q_own, :, lane]
    tc = send(tok.at[rows_of(1 - k)], t_dst, at_core)
    own_copy = pltpu.make_async_copy(tok.at[rows_of(k)], t_dst, rs.at[slots(1)])
    own_copy.start()
    dn_arrived = spread(dn, lambda h, zs, xs: D.at[:, h, zs, y, xs])

    un, uf = Gather(up_part(zh)), Gather(up_part(1 - zh))
    dN, dF = Gather(dn_part(zh)), Gather(dn_part(1 - zh))
    d0, d1, d2 = Gather(dn_last(0)), Gather(dn_last(1)), Gather(dn_last(2))

    own_copy.wait()
    tc.wait_recv()
    t_send(1, 1)
    r = T.at[zl, q_own, pl.ds(0, TA)]
    lo0 = send(r, r, at_lo)
    t_to_lo(z)
    up_arrived(zh)
    un.go(0)
    dn_arrived(zh)
    dN.go(0)
    lo0.wait_recv()
    t_send(0, 1)
    order()
    un.wait(0)
    un.go(1)
    dN.wait(0)
    dN.go(1)
    up_arrived(1 - zh)
    uf.go(0)
    un.wait(1)
    un.go(2)
    un.forward(held)
    uf.wait(0)
    uf.go(1)
    dn_arrived(1 - zh)
    dF.go(0)
    t_wait(1, 1)
    t_send(1, 2)
    t_wait(0, 1)
    t_send(0, 2)
    un.wait(2)
    un.forward(last)
    uf.wait(1)
    uf.go(2)
    uf.forward(held)
    t_wait(1, 2)
    t_send(1, 3)
    dN.wait(1)
    dF.wait(0)
    dF.go(1)
    t_wait(0, 2)
    t_send(0, 3)
    t_wait(1, 3)
    t_send(1, 4)
    t_wait(0, 3)
    t_send(0, 4)
    uf.wait(2)
    uf.forward(last)
    dF.wait(1)
    d0.go(2)
    d1.go(2)
    d2.go(2)
    d0.forward(held)
    d1.forward(held)
    d2.forward(held)
    t_wait(1, 4)
    t_wait(0, 4)
    for c in lo_live:
        c.wait_recv()
    un.wait("f")
    uf.wait("f")
    pre()
    lax.fori_loop(0, 4, act, 0)
    d0.wait(2)
    d0.forward(last)
    d1.wait(2)
    d1.forward(last)
    d0.wait("f")
    project(0)
    ring(0, 0)
    own(0)
    d2.wait(2)
    d2.forward(last)
    d1.wait("f")
    project(1)
    ring(1, 0)
    own(1)
    ring(0, 1)
    d2.wait("f")
    project(2)
    ring(2, 0)
    own(2)
    ring(1, 1)
    ring(0, 2)
    ring(2, 1)
    ring(1, 2)
    ring(0, 3)
    ring(2, 2)
    ring(1, 3)
    finish(0)
    ring(2, 3)
    finish(1)
    finish(2)
    out[...] = jnp.dot(V[...].reshape(160, 384), E[...], preferred_element_type=F32).astype(BF)
    for w in pending:
        w()


def local(tokens, up_weight, down_weight):
    vmem = pl.BlockSpec(memory_space=pltpu.VMEM)
    hbm = pl.BlockSpec(memory_space=pltpu.HBM)
    out = pl.pallas_call(
        body,
        out_shape=jax.ShapeDtypeStruct((160, 384), BF),
        in_specs=[hbm] * 3,
        out_specs=vmem,
        scratch_shapes=[
            pltpu.VMEM((4, 4, 80, 768), BF),
            pltpu.VMEM((2, 2, 4, 4, 96, 384), BF),
            pltpu.VMEM((3, 2, 2, 4, 4, 32, 384), BF),
            pltpu.VMEM((2, 320, 384), F32),
            pltpu.VMEM((320, 768), BF),
            pltpu.VMEM((3, 4, 2, 4, 80, 128), F32),
            pltpu.VMEM((24, 2, 2, 80, 128), BF),
            pltpu.VMEM((24, 2, 2, 80, 128), BF),
            pltpu.VMEM((3, 2, 2, 2, 80, 128), BF),
            pltpu.VMEM((3, 2, 2, 80, 128), BF),
            pltpu.VMEM((3, 2, 2, 80, 128), BF),
            pltpu.VMEM((2, 80, 384), BF),
            pltpu.VMEM((384, 384), BF),
            pltpu.SemaphoreType.DMA((SEMS,)),
            pltpu.SemaphoreType.DMA((SEMS,)),
        ],
        compiler_params=pltpu.CompilerParams(
            collective_id=0, has_side_effects=True, vmem_limit_bytes=63 << 20),
        name="ffn",
    )(tokens, up_weight, down_weight.T.reshape(3, 32, 1536))
    return out


def solution(mesh):
    return jax.shard_map(
        local,
        mesh=mesh,
        in_specs=(P("row", "col"), P("row", "col"), P("col", "row")),
        out_specs=P("row", "col"),
        check_vma=False,
    )
```

time: 563 us -> 82.9 us (0.15)
  blocking collectives: 305 us -> 0 us
  waiting for transfers between devices: 208 us -> 0 us
  Pallas kernels: 0 us -> 81.2 us
  matrix products: 15.9 us -> 0 us
  between operations: 13.1 us -> 0.01 us
  local copies, waits for them, and re-layouts: 12.6 us -> 1.56 us
  starting transfers between devices: 6.19 us -> 0 us
    all_gather x1 -> x0, blocking collectives: 305 us -> none  [local(): token_rows = lax.all_gather(tokens, 'col', axis=1, tiled=True)]
    all_gather x3 -> x0, waiting for transfers between devices: 207 us -> none  [the longest x1 172 us: local(): full_rows = lax.all_gather(down_weight, 'row', axis=1, tiled=True)]
    pallas_call x0 -> x1, Pallas kernels: none -> 81.2 us  [local(): pl.pallas_call(body, out_shape=jax.ShapeDtypeStruct((160, 384), BF), in_s...]
    dot_general x2 -> x0, matrix products: 15.9 us -> none  [the longest x1 8.16 us: add_panel(): return jnp.dot(left, piece, preferred_element_type=jnp.float32)]
    all_to_all x1 -> x0, local copies, waits for them, and re-layouts: 12.6 us -> none  [local(): lax.all_to_all(full_rows, 'col', split_axis=1, concat_axis=0, tiled=True)]
    all_to_all x1 -> x0, starting transfers between devices: 6.15 us -> none  [local(): lax.all_to_all(full_rows, 'col', split_axis=1, concat_axis=0, tiled=True)]
  transfers between devices with their start and end apart: 4 -> 0, of which waited for: 2 -> 0; matrix products, arithmetic and copies ran while one was open for 4% -> 0% of each run, Pallas kernels for 0% -> 0%
where the time goes in v2:
time: 82.9 us; the launch traced here: 82.8 us
  Pallas kernels  81.2 us (98%)
  local copies, waits for them, and re-layouts  1.56 us (2%)
    pallas_call x1, Pallas kernels, local(): pl.pallas_call(body, out_shape=jax.ShapeDtypeStruct((160, 384), BF), in_s...  81.2 us

profile of v2, /device:TPU:1, one launch (start us, length us, event | category | flops | bytes accessed | tf_op | source)
XLA Modules:
  0.0 82.8 jit_solution(16773701968640771676)
XLA Ops:
  0.0 81.2 %ffn.1 = bf16[160,384]{1,0:T(8,128)(2,1)} custom-call(bf16[160,384]{1,0:T(8,128)(2,1)} %tok.1, bf16[96,1536]{1,0:T(8,128)(2,1)} %up.1, bf16[3,32,1536]{2,1,0:T(8,128)(2,1)} %bitcast.3), custom_call_target="tpu_custom_call" | custom-call | tf_op jit(solution)/shard_map/ffn/pallas_call | solution.py:376
  81.2 1.6 %copy.5 = bf16[160,384]{1,0:T(8,128)(2,1)} copy(bf16[160,384]{1,0:T(8,128)(2,1)} %ffn.1) | data formatting | bytes 245760

commit v3 on v2

v3 whole, which is shorter than its diff:
```python
import jax
import jax.numpy as jnp
from jax import lax
from jax.experimental import pallas as pl
from jax.experimental.pallas import tpu as pltpu
from jax.sharding import PartitionSpec as P

MESH = pl.DeviceIdType.MESH
BF = jnp.bfloat16
F32 = jnp.float32
TA, TB = 32, 48
RA, RB = 80, 0
SEMS = 460
ORDER = (
    "uS1", "Tc", "uS0", "T11", "dS1", "un1", "dn11", "T0lo",
    "uf11", "un2", "uf01", "uf12", "dn12", "T01", "un3", "T12",
    "dS0", "df11", "Tl1", "uf1h", "Tl0", "dn01", "T02", "uf02",
    "unh", "uf13", "Tl2", "T13", "df01", "df12", "dn02", "T03",
    "T14", "uf03", "Tl3", "df02", "dn23x", "unl", "T04", "df23x",
    "uf1l", "dn03x", "Tl4", "uf0l", "df03x", "df13x", "uf0h", "dh0",
    "dn13x", "dl2", "dh1", "qre", "pre", "dl0", "p2", "r20",
    "dl1", "p0", "r00", "p1", "r10", "r21", "r01", "r11",
    "r22", "r02", "r12", "r23", "r03", "r13", "f2", "f0",
    "f1",
)


def dev(x, y, z, k):
    return ((z // 4) * 16 + y * 4 + x, (z % 4) * 2 + k)


def body(tok_h, up_h, dn_h, out, tok, up, dn, T, U, D, acc, H, O, SA, QA, FA, SO, OA, V, E, ss, rs, ls):
    row = lax.axis_index("row")
    col = lax.axis_index("col")
    x, y, zh = row % 4, (row // 4) % 4, row // 16
    zl, k = col // 2, col % 2
    z = 4 * zh + zl
    hi, lo = x // 2, x % 2
    yh, yl = y // 2, y % 2
    ya = 2 * yh + 1 - yl
    turn = ((x + 1) // 2) % 2
    x_lo = 2 * hi + 1 - lo

    def ring_z(n):
        return (z + 8 + n) % 8

    at_core = dev(x, y, z, 1 - k)
    at_lo = dev(x_lo, y, z, k)
    at_x = dev(3 - x, y, z, k)
    at_a = dev(x, ya, z, k)
    at_b = dev(x, 3 - y, z, k)
    at_z = (dev(x, y, ring_z(1), k), dev(x, y, ring_z(-1), k))

    loads = [pltpu.make_async_copy(a, b, ls.at[i]) for i, (a, b) in enumerate(((up_h, up), (tok_h, tok), (dn_h, dn)))]
    for c in loads:
        c.start()
    barrier = pltpu.get_barrier_semaphore()
    friends = [at_x, at_a, at_b]
    for n in (0, 4, 1, -1):
        for px in (x, x_lo):
            for pk in (k, 1 - k):
                if n or px is not x or pk is not k:
                    friends.append(dev(px, y, ring_z(n), pk))
    for f in friends:
        pl.semaphore_signal(barrier, inc=1, device_id=f, device_id_type=MESH)
    pl.semaphore_wait(barrier, len(friends))
    for c in loads:
        c.wait()

    count = [0]
    pending = []

    def slots(n):
        first = count[0]
        count[0] += n
        assert count[0] <= SEMS
        return first

    def copy(src, dst, to, i, j=None):
        return pltpu.make_async_remote_copy(
            src_ref=src, dst_ref=dst, send_sem=ss.at[i], recv_sem=rs.at[i if j is None else j],
            device_id=to, device_id_type=MESH)

    def send(src, dst, to, i=None, j=None):
        c = copy(src, dst, to, slots(1) if i is None else i, j)
        c.start()
        pending.append(c.wait_send)
        return c

    def landed(ref, i):
        pltpu.make_async_copy(ref, ref, rs.at[i]).wait()

    def spread(S, at):
        base = slots(4)
        far = zh + k - 2 * zh * k
        for g in (0, 1):
            for h in (0, 1):
                src = S.at[..., pl.ds((2 * g + h) * 384, 384)]
                dst = at(h, zh, x)
                to = dev(2 * hi + (1 - hi if g else hi), y, 4 * k + zl, h)
                own = (far == 0) & (turn == g) & (k == h)

                def c(src=src, dst=dst, to=to, i=base + 2 * g + h):
                    return copy(src, dst, to, i, base + 2 * far + lo)

                @pl.when(own)
                def _():
                    pltpu.make_async_copy(src, dst, rs.at[base + 2 * far + lo]).start()

                @pl.when(jnp.logical_not(own))
                def _():
                    c().start()

                def done(own=own, c=c):
                    @pl.when(jnp.logical_not(own))
                    def _():
                        c().wait_send()
                pending.append(done)

        def arrived(zs):
            off = zs + zh - 2 * zs * zh
            for l in (0, 1):
                landed(at(k, zs, 2 * hi + l), base + 2 * off + l)
        return arrived

    pair, other = pl.ds(2 * hi, 2), pl.ds(2 - 2 * hi, 2)
    ypair, yother = pl.ds(2 * yh, 2), pl.ds(2 - 2 * yh, 2)
    every = pl.ds(0, 4)
    plan = (
        ((at_x, 0, ((y, pair),)), (at_a, 1, ((y, pair),)), (at_b, 2, ((y, pair),))),
        ((at_a, 0, ((y, every),)), (at_b, 1, ((ypair, pair),)), (at_x, 2, ((y, pair), (3 - y, pair)))),
        ((at_b, 0, ((ypair, every),)), (at_x, 1, ((every, pair),)), (at_a, 2, ((y, every), (3 - y, every)))),
    )
    held = tuple((p, s) for _, p, s in plan[2])
    last = ((0, ((yother, every),)), (1, ((every, other),)), (2, ((ya, every), (3 - ya, every))))

    class Gather:
        def __init__(self, part):
            self.part, self.live = part, {}

        def go(self, step):
            rs_ = [(to, self.part(ys, xs, p)) for to, p, sets in plan[step] for ys, xs in sets]
            self.live[step] = [send(r, r, to) for to, r in rs_]

        def wait(self, step):
            for c in self.live.pop(step, ()):
                c.wait_recv()

        def forward(self, what):
            rs_ = [self.part(ys, xs, p) for p, sets in what for ys, xs in sets]
            self.live["f"] = self.live.get("f", []) + [send(r, r, at_core) for r in rs_]

    def up_part(zs, rows=slice(None)):
        return lambda ys, xs, p: U.at[k, zs, ys, xs, p, rows]

    phases = (0, pl.ds(1, 2))

    def dn_part(g, zs):
        return lambda ys, xs, p: D.at[phases[g], k, zs, ys, xs, :, pl.ds(128 * p, 128)]

    def dn_last(b, zs):
        return lambda ys, xs, p: D.at[b, k, zs, ys, xs, :, pl.ds(128 * p, 128)]

    def most(st, dr):
        return 4 if st == dr else 3

    def t_slice(zo, st):
        if st == 0:
            return T.at[zo % 4, pl.ds(2 * (zo // 4), 2), pl.ds(0, TA)]
        return T.at[zo % 4, 2 * (zo // 4) + lo, pl.ds(TA, TB)]

    sent, lo_live, seen = {}, [], set()

    def need(*name):
        if name not in seen:
            seen.add(name)
            sent[name].wait_recv()

    def t_origin(dr, d):
        return ring_z(-d if dr == 0 else d)

    def t_send(st, d):
        for dr in (0, 1):
            if d <= most(st, dr):
                if d > 1:
                    need("t", st, dr, d - 1)
                r = t_slice(t_origin(dr, d - 1), st)
                sent["t", st, dr, d] = send(r, r, at_z[dr])

    def t_lo(d):
        for dr in (0, 1):
            if d <= most(1, dr):
                need("t", 1, dr, d)
                t_to_lo(t_origin(dr, d))

    def t_to_lo(zo):
        r = t_slice(zo, 1)
        lo_live.append(send(r, r, at_lo))

    def project(b):
        w = jnp.concatenate([D[b, h].reshape(1024, 384) for h in (0, 1)], axis=1)
        o = lax.dot_general(H[...], w, (((1,), (1,)), ((), ())), preferred_element_type=F32)
        for j in range(8):
            O[b, j // 2, j % 2] = o[:, 128 * j:128 * j + 128].reshape(4, 80, 128)

    ring_base = slots(48)
    last_send, last_recv = slots(36), slots(36)
    own_send, own_recv = slots(12), slots(15)
    l_base = slots(24)
    cut = (slice(0, RA), slice(RA, 80))

    def far_dir(b, st, dr):
        return (b + st) % 2 == dr

    def term(b, st, t):
        return O[b, t % 4, :, pl.ds(2 * (t // 4), 2)]

    def ring_copies(b, st, dr, d):
        m = (b * 2 + dr) * 4
        S, Q = SA, QA
        src, i = S.at[m + d - 1], ring_base + 24 * st + m
        if d > 1:
            return [copy(src, Q.at[m + d - 1], at_z[dr], i + d - 1)]
        zt = ring_z(1 if dr == 0 else -1)
        if True:
            return [copy(src.at[c, l], FA.at[b, dr, k, lo], dev(2 * hi + l, y, zt, c),
                         last_send + m + 2 * c + l, last_recv + m + 2 * k + lo)
                    for c in (0, 1) for l in (0, 1)]

    def ring(b, st, step):
        S, Q = SA, QA
        for dr in (0, 1):
            d = (4 if far_dir(b, st, dr) else 3) - step
            if d == 0:
                continue
            m = (b * 2 + dr) * 4
            v = term(b, st, ring_z(d if dr == 0 else -d))
            if step:
                ring_copies(b, st, dr, d + 1)[0].wait_recv()
                v = v + Q[m + d].astype(F32)
            S[m + d - 1] = v.astype(BF)
            for c in ring_copies(b, st, dr, d):
                c.start()
                pending.append(c.wait_send)

    def own(b):
        SO[b] = O[b, zl, :, pl.ds(2 * zh, 2), 0:RA].astype(BF)
        for i, (l, c) in enumerate(((lo, 1 - k), (1 - lo, k), (1 - lo, 1 - k))):
            send(SO.at[b, c, l], OA.at[b, k, lo], dev(2 * hi + l, y, z, c), own_send + 4 * b + i, own_recv + 5 * b + 2 * k + lo)

    def up32(r):
        return r.astype(F32)

    def finish(b):
        for l in (0, 1):
            landed(OA.at[b, 1 - k, l], own_recv + 5 * b + 2 * (1 - k) + l)
        landed(OA.at[b, k, 1 - lo], own_recv + 5 * b + 2 * k + 1 - lo)
        for kk in (1 - k, k):
            if kk is k:
                v = O[b, zl, k, 2 * zh + lo, 0:RA] + up32(OA[b, k, 1 - lo])
            else:
                v = up32(OA[b, kk, 0]) + up32(OA[b, kk, 1])
            for dr in (0, 1):
                for l in (0, 1):
                    landed(FA.at[b, dr, kk, l], last_recv + (b * 2 + dr) * 4 + 2 * kk + l)
                    v = v + up32(FA[b, dr, kk, l])
            V[kk, 0:RA, 128 * b:128 * b + 128] = v.astype(BF)

    def order():
        i = lax.broadcasted_iota(jnp.int32, (384, 384), 0)
        j = lax.broadcasted_iota(jnp.int32, (384, 384), 1)
        E[...] = (j == 96 * ((i % 128) // 32) + 32 * (i // 128) + i % 32).astype(F32).astype(BF)

    def pre(zs, first):
        for h in (0, 1):
            v = None if first else acc[h]
            for j in (0, 1):
                o = jnp.dot(T[2 * zs + j].reshape(320, 768), U[h, zs, 2 * j:2 * j + 2].reshape(768, 384),
                            preferred_element_type=F32)
                v = o if v is None else v + o
            acc[h] = v

    def act(j, carry):
        r = pl.ds(pl.multiple_of(j * 80, 16), 80)
        for h in (0, 1):
            v = acc[h, r, :]
            H[r, h * 384:(h + 1) * 384] = (v * (1.0 + lax.erf(v * 0.7071067811865476)) * 0.5).astype(BF)
        return carry

    rows_of = lambda c: pl.ds(pl.multiple_of(c * 80, 16), 80)
    lane = pl.ds(pl.multiple_of(k * 384, 128), 384)
    q_own = 2 * zh + lo
    t_dst = T.at[zl, q_own, :, lane]
    own_copy = pltpu.make_async_copy(tok.at[rows_of(k)], t_dst, rs.at[slots(1)])
    arrived = {}
    halves = (pl.ds(0, 16), pl.ds(16, 16))
    un = Gather(up_part(zh))
    uf = [Gather(up_part(1 - zh, r)) for r in halves]
    dn_g = [Gather(dn_part(g, zh)) for g in (0, 1)]
    df_g = [Gather(dn_part(g, 1 - zh)) for g in (0, 1)]
    dh_g = [Gather(dn_part(g, pl.ds(0, 2))) for g in (0, 1)]
    near = [Gather(dn_last(b, zh)) for b in range(3)]
    far = [Gather(dn_last(b, 1 - zh)) for b in range(3)]
    both = [Gather(dn_last(b, pl.ds(0, 2))) for b in range(3)]

    def ready(what, zs):
        if (what, zs is zh) not in seen:
            seen.add((what, zs is zh))
            arrived[what](zs)

    def tokens_in():
        sent["tc",] = send(tok.at[rows_of(1 - k)], t_dst, at_core)
        own_copy.start()

    def tokens_here():
        if "own" not in seen:
            seen.add("own")
            own_copy.wait()
        need("tc")

    def gather_step(G, what, zs, step):
        if step == 0:
            ready(what, zs)
        else:
            G.wait(step - 1)
        G.go(step)

    def tokens_all():
        if "all" not in seen:
            seen.add("all")
            for c in lo_live:
                c.wait_recv()
            for dr in (0, 1):
                need("t", 0, dr, most(0, dr))

    def hidden():
        for G in uf:
            G.wait("f")
        pre(1 - zh, False)
        lax.fori_loop(0, 4, act, 0)

    def run(op):
        kind, n = op[0], op[1:]
        if op[:2] == "uS":
            i = int(op[2])
            arrived["u", i] = spread(up.at[:, halves[i]], lambda h, zs, xs: U.at[h, zs, y, xs, :, halves[i]])
        elif op == "Tc":
            tokens_in()
        elif op == "T0lo":
            tokens_here()
            r = T.at[zl, q_own, pl.ds(0, TA)]
            sent["lo",] = send(r, r, at_lo)
        elif op == "Tl0":
            tokens_here()
            t_to_lo(z)
        elif op[:2] == "Tl":
            t_lo(int(op[2]))
        elif kind == "T":
            if op == "T01":
                need("lo")
            if op == "T11":
                tokens_here()
            t_send(int(op[1]), int(op[2]))
        elif op[:2] == "dS":
            g = int(op[2])
            arrived["d", g] = spread(dn.at[phases[g]], lambda h, zs, xs: D.at[phases[g], h, zs, y, xs])
        elif kind == "u":
            i = 0 if op[1] == "n" else int(op[2])
            G, zs, what = (un, zh, op[2:]) if op[1] == "n" else (uf[i], 1 - zh, op[3:])
            if what == "h":
                G.wait(1)
                G.forward(held)
            elif what == "l":
                G.wait(2)
                G.forward(last)
            else:
                if what == "1":
                    for j in ((0, 1) if op[1] == "n" else (i,)):
                        ready(("u", j), zs)
                else:
                    G.wait(int(what) - 2)
                G.go(int(what) - 1)
        elif op == "qre":
            tokens_all()
            un.wait("f")
            pre(zh, True)
        elif op[:2] == "dh":
            g = int(op[2])
            dn_g[g].wait(1)
            df_g[g].wait(1)
            dh_g[g].forward(held)
        elif op[:2] == "dl":
            b = int(op[2])
            near[b].wait(2)
            far[b].wait(2)
            both[b].forward(last)
        elif kind == "d":
            i = int(op[2])
            G, zs, L = (dn_g, zh, near) if op[1] == "n" else (df_g, 1 - zh, far)
            if op[3:] == "3x":
                G[min(i, 1)].wait(1)
                L[i].go(2)
            else:
                gather_step(G[i], ("d", i), zs, int(op[3]) - 1)
        elif op == "pre":
            hidden()
        elif kind == "p":
            b = int(n)
            dh_g[min(b, 1)].wait("f")
            both[b].wait("f")
            project(b)
        elif kind == "r":
            ring(int(n[0]), 0, int(n[1]))
            if n[1] == "0":
                own(int(n[0]))
        elif kind == "f":
            finish(int(n))

    for op in ORDER:
        if op == "un1":
            order()
        run(op)
    out[...] = jnp.dot(V[...].reshape(160, 384), E[...], preferred_element_type=F32).astype(BF)
    for w in pending:
        w()


def local(tokens, up_weight, down_weight):
    vmem = pl.BlockSpec(memory_space=pltpu.VMEM)
    hbm = pl.BlockSpec(memory_space=pltpu.HBM)
    out = pl.pallas_call(
        body,
        out_shape=jax.ShapeDtypeStruct((160, 384), BF),
        in_specs=[hbm] * 3,
        out_specs=vmem,
        scratch_shapes=[
            pltpu.VMEM((160, 384), BF),
            pltpu.VMEM((3, 32, 1536), BF),
            pltpu.VMEM((3, 32, 1536), BF),
            pltpu.VMEM((4, 4, 80, 768), BF),
            pltpu.VMEM((2, 2, 4, 4, 3, 32, 384), BF),
            pltpu.VMEM((3, 2, 2, 4, 4, 32, 384), BF),
            pltpu.VMEM((2, 320, 384), F32),
            pltpu.VMEM((320, 768), BF),
            pltpu.VMEM((3, 4, 2, 4, 80, 128), F32),
            pltpu.VMEM((24, 2, 2, RA, 128), BF),
            pltpu.VMEM((24, 2, 2, RA, 128), BF),
            pltpu.VMEM((3, 2, 2, 2, RA, 128), BF),
            pltpu.VMEM((3, 2, 2, RA, 128), BF),
            pltpu.VMEM((3, 2, 2, RA, 128), BF),
            pltpu.VMEM((2, 80, 384), BF),
            pltpu.VMEM((384, 384), BF),
            pltpu.SemaphoreType.DMA((SEMS,)),
            pltpu.SemaphoreType.DMA((SEMS,)),
            pltpu.SemaphoreType.DMA((3,)),
        ],
        compiler_params=pltpu.CompilerParams(
            collective_id=0, has_side_effects=True, vmem_limit_bytes=55040 << 10),
        name="ffn",
    )(tokens, up_weight.reshape(3, 32, 1536), down_weight.T.reshape(3, 32, 1536))
    return out


def solution(mesh):
    return jax.shard_map(
        local,
        mesh=mesh,
        in_specs=(P("row", "col"), P("row", "col"), P("col", "row")),
        out_specs=P("row", "col"),
        check_vma=False,
    )
```

time: 82.9 us -> 79.1 us (0.954)
  Pallas kernels: 81.2 us -> 78.3 us
  local copies, waits for them, and re-layouts: 1.56 us -> 0.65 us
    pallas_call x1, Pallas kernels: 81.2 us -> 78.3 us  [local(): pl.pallas_call(body, out_shape=jax.ShapeDtypeStruct((160, 384), BF), in_s...]
    unnamed x1, local copies, waits for them, and re-layouts: 1.56 us -> 0.65 us
where the time goes in v3:
time: 79.1 us; the launch traced here: 79 us
  Pallas kernels  78.3 us (99%)
    pallas_call x1, Pallas kernels, local(): pl.pallas_call(body, out_shape=jax.ShapeDtypeStruct((160, 384), BF), in_s...  78.3 us

profile of v3, /device:TPU:1, one launch (start us, length us, event | category | flops | bytes accessed | tf_op | source)
XLA Modules:
  0.0 79.0 jit_solution(12925197469472136722)
XLA Ops:
  0.0 78.3 %ffn.1 = bf16[160,384]{1,0:T(8,128)(2,1)S(1)} custom-call(bf16[160,384]{1,0:T(8,128)(2,1)} %tok_h.1, bf16[3,32,1536]{2,1,0:T(8,128)(2,1)} %bitcast.4, bf16[3,32,1536]{2,1,0:T(8,128)(2,1)} %bitcast.5), custom_call_target="tpu_custom_call" | custom-call | tf_op jit(solution)/shard_map/ffn/pallas_call | solution.py:431
  78.3 0.7 copy.5

commit v4 on v3

--- a/solution.py
+++ b/solution.py
@@ -411,15 +411,17 @@
             project(b)
         elif kind == "r":
             ring(int(n[0]), 0, int(n[1]))
-            if n[1] == "0":
-                own(int(n[0]))
         elif kind == "f":
             finish(int(n))
 
+    starts = [op for op in ORDER if op[0] == "r" and op[2] == "0"]
     for op in ORDER:
         if op == "un1":
             order()
         run(op)
+        if op == starts[-1]:
+            for first in starts:
+                own(int(first[1]))
     out[...] = jnp.dot(V[...].reshape(160, 384), E[...], preferred_element_type=F32).astype(BF)
     for w in pending:
         w()

time: 79.1 us -> 79.1 us (level)
  no operation moved by 1% of the time
where the time goes in v4:
time: 79.1 us; the launch traced here: 79 us
  Pallas kernels  78.3 us (99%)
    pallas_call x1, Pallas kernels, local(): pl.pallas_call(body, out_shape=jax.ShapeDtypeStruct((160, 384), BF), in_s...  78.3 us

profile of v4, /device:TPU:1, one launch (start us, length us, event | category | flops | bytes accessed | tf_op | source)
XLA Modules:
  0.0 79.0 jit_solution(5671798061832408126)
XLA Ops:
  0.0 78.3 %ffn.1 = bf16[160,384]{1,0:T(8,128)(2,1)S(1)} custom-call(bf16[160,384]{1,0:T(8,128)(2,1)} %tok_h.1, bf16[3,32,1536]{2,1,0:T(8,128)(2,1)} %bitcast.4, bf16[3,32,1536]{2,1,0:T(8,128)(2,1)} %bitcast.5), custom_call_target="tpu_custom_call" | custom-call | tf_op jit(solution)/shard_map/ffn/pallas_call | solution.py:433
  78.3 0.7 copy.5

commit v5 on v4

--- a/solution.py
+++ b/solution.py
@@ -271,21 +271,23 @@
         j = lax.broadcasted_iota(jnp.int32, (384, 384), 1)
         E[...] = (j == 96 * ((i % 128) // 32) + 32 * (i // 128) + i % 32).astype(F32).astype(BF)
 
-    def pre(zs, first):
-        for h in (0, 1):
-            v = None if first else acc[h]
-            for j in (0, 1):
-                o = jnp.dot(T[2 * zs + j].reshape(320, 768), U[h, zs, 2 * j:2 * j + 2].reshape(768, 384),
-                            preferred_element_type=F32)
-                v = o if v is None else v + o
-            acc[h] = v
-
-    def act(j, carry):
-        r = pl.ds(pl.multiple_of(j * 80, 16), 80)
-        for h in (0, 1):
+    def pre(zs, h, first):
+        v = None if first else acc[h]
+        for j in (0, 1):
+            o = jnp.dot(T[2 * zs + j].reshape(320, 768), U[h, zs, 2 * j:2 * j + 2].reshape(768, 384),
+                        preferred_element_type=F32)
+            v = o if v is None else v + o
+        acc[h] = v
+
+    def act(h):
+        lanes = pl.ds(pl.multiple_of(h * 384, 128), 384)
+
+        def step(j, carry):
+            r = pl.ds(pl.multiple_of(j * 80, 16), 80)
             v = acc[h, r, :]
-            H[r, h * 384:(h + 1) * 384] = (v * (1.0 + lax.erf(v * 0.7071067811865476)) * 0.5).astype(BF)
-        return carry
+            H[r, lanes] = (v * (1.0 + lax.erf(v * 0.7071067811865476)) * 0.5).astype(BF)
+            return carry
+        lax.fori_loop(0, 4, step, 0)
 
     rows_of = lambda c: pl.ds(pl.multiple_of(c * 80, 16), 80)
     lane = pl.ds(pl.multiple_of(k * 384, 128), 384)
@@ -334,10 +336,12 @@
                 need("t", 0, dr, most(0, dr))
 
     def hidden():
+        pre(1 - zh, k, False)
+        act(k)
         for G in uf:
             G.wait("f")
-        pre(1 - zh, False)
-        lax.fori_loop(0, 4, act, 0)
+        pre(1 - zh, 1 - k, False)
+        act(1 - k)
 
     def run(op):
         kind, n = op[0], op[1:]
@@ -383,7 +387,8 @@
         elif op == "qre":
             tokens_all()
             un.wait("f")
-            pre(zh, True)
+            for h in (0, 1):
+                pre(zh, h, True)
         elif op[:2] == "dh":
             g = int(op[2])
             dn_g[g].wait(1)

time: 79.1 us -> 79.1 us (level)
  no operation moved by 1% of the time
where the time goes in v5:
time: 79.1 us; the launch traced here: 79 us
  Pallas kernels  78.3 us (99%)
    pallas_call x1, Pallas kernels, local(): pl.pallas_call(body, out_shape=jax.ShapeDtypeStruct((160, 384), BF), in_s...  78.3 us

profile of v5, /device:TPU:1, one launch (start us, length us, event | category | flops | bytes accessed | tf_op | source)
XLA Modules:
  0.0 79.0 jit_solution(4476251434896375279)
XLA Ops:
  0.0 78.3 %ffn.1 = bf16[160,384]{1,0:T(8,128)(2,1)S(1)} custom-call(bf16[160,384]{1,0:T(8,128)(2,1)} %tok_h.1, bf16[3,32,1536]{2,1,0:T(8,128)(2,1)} %bitcast.4, bf16[3,32,1536]{2,1,0:T(8,128)(2,1)} %bitcast.5), custom_call_target="tpu_custom_call" | custom-call | tf_op jit(solution)/shard_map/ffn/pallas_call | solution.py:438
  78.3 0.7 copy.5
